TPU v7x, 32 devices: a whole 2x2x4 slice. The times are simulated.
32 devices in a mesh: section: 1, seq: 16 (over z, y, x), mp: 2 (over core).
Axes of the slice: x: 2, y: 2, z: 4, core: 2. Of those that a mesh axis runs over, the one named last changes fastest.
Arguments:
- hidden_in: bfloat16 [4096, 5376], P('seq'), may hold values from -30 to 30
- query_weight: bfloat16 [1, 5376, 2048], P('section', 'seq', 'mp'), may hold values from -0.078125 to 0.078125
- key_weight: bfloat16 [1, 5376, 1024], P('section', 'seq', 'mp'), may hold values from -0.078125 to 0.078125
- value_weight: bfloat16 [1, 5376, 1024], P('section', 'seq', 'mp'), may hold values from -0.078125 to 0.078125
- output_weight: bfloat16 [1, 2048, 5376], P('section', 'mp', 'seq'), may hold values from -0.5524272 to 0.5524272
- input_gain: bfloat16 [1, 5376], P('section'), may hold values from 0.099609375 to 1.8984375
- post_gain: bfloat16 [1, 5376], P('section', 'mp'), may hold values from 0.099609375 to 1.8984375
Outputs:
- hidden_out: bfloat16 [1, 4096, 5376], P('section', 'seq', 'mp')
All inputs are finite; a program needn't handle non-finite values.
Results may differ from a plain program's by a relative error of at most 0.013.
Values may be sent and summed in bfloat16 or wider, within the bound.
A program may use at most 128 MiB of HBM per device.

v0:
```python
import math
import jax
import jax.numpy as jnp
from jax import lax
from jax.sharding import PartitionSpec as P

HEADS = 16
KV_HEADS = 8
HEAD_DIM = 128
WINDOW = 1024
QSCALE = 168
NORM_EPS = 1e-06


def from_behind(block, axis, distance):
    devices = range(lax.axis_size(axis))
    route = [(i - distance, i) for i in devices if i - distance in devices]
    return lax.ppermute(block, axis, route)


def rope_tables(positions, head_size):
    half_dim = head_size // 2
    frequency = jnp.exp(
        -math.log(10000.0) * (2.0 * jnp.arange(half_dim, dtype=jnp.float32)) / head_size
    )
    angles = positions.astype(jnp.float32)[:, None] * frequency[None, :]
    return (jnp.cos(angles), jnp.sin(angles))


def norm_rotate(values, cosine, sine_table):
    scaled = values * lax.rsqrt(jnp.mean(values * values, axis=-1, keepdims=True) + NORM_EPS)
    half_dim = scaled.shape[-1] // 2
    leading = scaled[..., :half_dim]
    trailing = scaled[..., half_dim:]
    cosine = cosine[:, None, :]
    sine_table = sine_table[:, None, :]
    rotated = jnp.concatenate(
        [leading * cosine - trailing * sine_table, trailing * cosine + leading * sine_table],
        axis=-1,
    )
    return rotated.astype(jnp.bfloat16)


def body(hidden_in, query_weight, key_weight, value_weight, output_weight, input_gain, post_gain):
    row_count = hidden_in.shape[0]
    model_width = hidden_in.shape[1]
    half_width = post_gain.shape[1]
    core_index = lax.axis_index("mp")
    shard_index = lax.axis_index("seq")
    section_index = lax.axis_index("section")
    query_full, key_full, value_full = (
        lax.all_gather(query_weight[0], "seq", axis=0, tiled=True),
        lax.all_gather(key_weight[0], "seq", axis=0, tiled=True),
        lax.all_gather(value_weight[0], "seq", axis=0, tiled=True),
    )
    output_full = lax.all_gather(output_weight[0], "seq", axis=1, tiled=True)
    gain_first = input_gain[0].astype(jnp.float32)
    gain_second = post_gain[0].astype(jnp.float32)
    group_size = HEADS // KV_HEADS
    query_heads_local = query_full.shape[1] // HEAD_DIM
    local_heads = key_full.shape[1] // HEAD_DIM
    reach_shards = (WINDOW + row_count - 2) // row_count
    score_scale = 1.0 / math.sqrt(QSCALE)
    positions = shard_index * row_count + jnp.arange(row_count, dtype=jnp.int32)
    cosine, sine_table = rope_tables(positions, HEAD_DIM)
    key_positions = (
        shard_index * row_count
        - reach_shards * row_count
        + jnp.arange((reach_shards + 1) * row_count, dtype=jnp.int32)
    )
    distance = positions[:, None] - key_positions[None, :]
    visible = ((distance >= 0) & (distance < WINDOW) & (key_positions[None, :] >= 0)).astype(
        jnp.float32
    )

    def project_rows(full_rows):
        rows_float = full_rows.astype(jnp.float32)
        normed = (
            rows_float
            * lax.rsqrt(jnp.mean(rows_float * rows_float, axis=1, keepdims=True) + NORM_EPS)
            * gain_first
        ).astype(jnp.bfloat16)
        queries = jnp.dot(normed, query_full, preferred_element_type=jnp.float32)
        keys_raw = jnp.dot(normed, key_full, preferred_element_type=jnp.float32)
        values_raw = jnp.dot(normed, value_full, preferred_element_type=jnp.float32)
        query_heads = norm_rotate(
            queries.reshape(row_count, query_heads_local, HEAD_DIM), cosine, sine_table
        )
        key_heads = norm_rotate(
            keys_raw.reshape(row_count, local_heads, HEAD_DIM), cosine, sine_table
        )
        key_value = jnp.concatenate(
            [key_heads.reshape(row_count, -1), values_raw.astype(jnp.bfloat16)], axis=1
        )
        return (query_heads, key_value)

    def skip_rows(full_rows):
        return (
            jnp.zeros((row_count, query_heads_local, HEAD_DIM), jnp.bfloat16),
            jnp.zeros((row_count, 2 * local_heads * HEAD_DIM), jnp.bfloat16),
        )

    def attend_rows(query_heads, window_rows):
        window_count = window_rows.shape[0]
        key_block = window_rows[:, : local_heads * HEAD_DIM].reshape(
            window_count, local_heads, HEAD_DIM
        )
        value_block = window_rows[:, local_heads * HEAD_DIM :].reshape(
            window_count, local_heads, HEAD_DIM
        )
        grouped = query_heads.reshape(row_count, local_heads, group_size, HEAD_DIM)
        scores = (
            jnp.einsum("tkgd,skd->kgts", grouped, key_block, preferred_element_type=jnp.float32)
            * score_scale
        )
        weights_raw = jnp.exp(scores) * visible
        softmax_weights = (weights_raw / jnp.sum(weights_raw, axis=-1, keepdims=True)).astype(
            jnp.bfloat16
        )
        attended = jnp.einsum(
            "kgts,skd->tkgd", softmax_weights, value_block, preferred_element_type=jnp.float32
        )
        attended = attended.astype(jnp.bfloat16).reshape(row_count, -1)
        return jnp.dot(attended, output_full, preferred_element_type=jnp.float32)

    def skip_attend(query_heads, window_rows):
        return jnp.zeros((row_count, model_width), jnp.float32)

    def attend_layer(full_rows, residual_half, active):
        query_heads, key_value = lax.cond(active, project_rows, skip_rows, full_rows)
        pieces = [key_value]
        carried = key_value
        for offset in range(reach_shards):
            carried = from_behind(carried, "seq", 1)
            pieces = [carried] + pieces
        window_rows = jnp.concatenate(pieces, axis=0)
        partial_value = lax.cond(active, attend_rows, skip_attend, query_heads, window_rows)
        summed = lax.psum_scatter(
            partial_value.astype(jnp.bfloat16), "mp", scatter_dimension=1, tiled=True
        ).astype(jnp.float32)
        squares = lax.psum(jnp.sum(summed * summed, axis=1, keepdims=True), "mp")
        branch = summed * lax.rsqrt(squares / model_width + NORM_EPS) * gain_second
        return (residual_half.astype(jnp.float32) + branch).astype(jnp.bfloat16)

    own_half = lax.dynamic_slice_in_dim(hidden_in, core_index * half_width, half_width, 1)
    layer_one = attend_layer(hidden_in, own_half, section_index == 0)
    arrived = from_behind(layer_one, "section", 1)
    full_rows = lax.all_gather(arrived, "mp", axis=1, tiled=True)
    layer_two = attend_layer(full_rows, arrived, section_index == 1)
    result = jnp.where(section_index == 0, layer_one, layer_two)
    return result[None]


def solution(mesh):
    placed = (
        P("seq", None),
        P("section", "seq", "mp"),
        P("section", "seq", "mp"),
        P("section", "seq", "mp"),
        P("section", "mp", "seq"),
        P("section", None),
        P("section", "mp"),
    )
    return jax.shard_map(
        body, mesh=mesh, in_specs=placed, out_specs=P("section", "seq", "mp"), check_vma=False
    )
```

profile of v0, /device:TPU:0, one launch (start us, length us, event | category | flops | bytes accessed | tf_op | source)
XLA Modules:
  0.0 530.9 jit_solution(8867680530757714097)
XLA Ops:
  6.5 0.0 all-gather.9.cloned.1.call-start
  6.5 0.7 all-gather.9.cloned.1.call-update
  7.3 0.0 all-gather.11.cloned.1.call-start
  7.3 0.7 all-gather.11.cloned.1.call-update
  8.0 0.0 all-gather.13.cloned.1.call-start
  8.1 0.7 all-gather.13.cloned.1.call-update
  8.7 0.0 all-gather.15.cloned.1.call-start
  8.8 0.5 all-gather.15.cloned.1.call-update
  9.3 0.0 reduce-scatter.4.cloned.1.call-start
  9.4 0.8 convert_reduce_fusion
  10.2 0.0 copy-start.3
  10.2 2.4 fusion.8
  12.6 0.5 multiply_cosine_fusion
  13.2 86.9 %all-gather.9.cloned.1.call-done = bf16[1,5376,512]{2,1,0:T(8,128)(2,1)} async-done(((bf16[1,336,512]{2,1,0:T(8,128)(2,1)}), bf16[1,5376,512]{2,1,0:T(8,128)(2,1)}) %all-gather.9.cloned.1.call-update) | async-done | bytes 5505040 | tf_op jit(solution)/shard_map/all_gather | solution.py:53
  100.1 0.0 copy-done.3
  100.1 0.0 copy-done
  100.1 5.0 fusion.13
  105.1 1.2 reshape.109
  106.3 0.3 multiply_reduce_fusion.1
  106.7 0.3 broadcast_multiply_fusion.1
  107.0 0.5 subtract_convert_fusion.1
  107.5 0.4 pad_maximum_fusion.1
  108.0 80.6 %all-gather.11.cloned.1.call-done = bf16[1,5376,512]{2,1,0:T(8,128)(2,1)} async-done(((bf16[1,336,512]{2,1,0:T(8,128)(2,1)}), bf16[1,5376,512]{2,1,0:T(8,128)(2,1)}) %all-gather.11.cloned.1.call-update) | async-done | bytes 5505040 | tf_op jit(solution)/shard_map/all_gather | solution.py:54
  188.6 4.2 fusion.30
  192.8 0.1 pad_maximum_fusion
  192.9 3.4 collective-permute-start
  196.3 15.0 %collective-permute-done = bf16[256,1024]{1,0:T(8,128)(2,1)S(1)} collective-permute-done((bf16[256,1024]{1,0:T(8,128)(2,1)S(1)}, bf16[256,1024]{1,0:T(8,128)(2,1)S(1)}, u32[]{:S(2)}, u32[]{:S(2)}) %collective-permute-start) | collective-permute-done | bytes 524320 | tf_op jit(solution)/shard_map/ppermute | solution.py:18
  211.3 4.4 collective-permute-start.1
  215.7 9.3 %collective-permute-done.1 = bf16[256,1024]{1,0:T(8,128)(2,1)S(1)} collective-permute-done((bf16[256,1024]{1,0:T(8,128)(2,1)S(1)}, bf16[256,1024]{1,0:T(8,128)(2,1)S(1)}, u32[]{:S(2)}, u32[]{:S(2)}) %collective-permute-start.1) | collective-permute-done | bytes 524320 | tf_op jit(solution)/shard_map/ppermute | solution.py:18
  225.0 5.2 collective-permute-start.2
  230.2 19.9 %collective-permute-done.2 = bf16[256,1024]{1,0:T(8,128)(2,1)} collective-permute-done((bf16[256,1024]{1,0:T(8,128)(2,1)S(1)}, bf16[256,1024]{1,0:T(8,128)(2,1)}, u32[]{:S(2)}, u32[]{:S(2)}) %collective-permute-start.2) | collective-permute-done | bytes 524320 | tf_op jit(solution)/shard_map/ppermute | solution.py:18
  250.1 4.7 collective-permute-start.3
  254.8 0.4 fusion.28
  255.2 13.6 %collective-permute-done.3 = bf16[256,1024]{1,0:T(8,128)(2,1)S(1)} collective-permute-done((bf16[256,1024]{1,0:T(8,128)(2,1)}, bf16[256,1024]{1,0:T(8,128)(2,1)S(1)}, u32[]{:S(2)}, u32[]{:S(2)}) %collective-permute-start.3) | collective-permute-done | bytes 524320 | tf_op jit(solution)/shard_map/ppermute | solution.py:18
  268.9 1.1 constant_dynamic-update-slice_fusion.3
  270.0 0.1 constant_dynamic-update-slice_fusion
  270.1 1.2 fusion.42
  271.3 3.6 reshape.110
  274.9 1.4 copy.44
  276.3 76.1 %all-gather.13.cloned.1.call-done = bf16[1,5376,1024]{2,1,0:T(8,128)(2,1)} async-done(((bf16[1,336,1024]{2,1,0:T(8,128)(2,1)}), bf16[1,5376,1024]{2,1,0:T(8,128)(2,1)}) %all-gather.13.cloned.1.call-update) | async-done | bytes 11010064 | tf_op jit(solution)/shard_map/all_gather | solution.py:52
  352.4 0.0 copy-done.4
  352.4 6.7 %fusion.21 = f32[32,8,8,128]{3,1,2,0:T(8,128)S(1)} fusion(bf16[1,5376,1024]{2,1,0:T(8,128)(2,1)} %all-gather.13.cloned.1.call-done, bf16[256,5376]{1,0:T(8,128)(2,1)} %param.7, f32[5376]{0:T(1024)S(1)} %copy-done.4, f32[256]{0:T(256)S(1)} %add_rsqrt_fusion.3), kind=kOutput, calls=%fused_computation.27 | convolution fusion | flops 2824077312 | bytes 14833664 | tf_op jit(solution)/shard_map/cond/branch_1_fun/dot_general | solution.py:83
  359.2 0.2 copy.48
  359.4 0.3 multiply_reduce_fusion
  359.7 0.1 copy.32
  359.8 0.2 copy.33
  359.9 0.3 broadcast_multiply_fusion
  360.3 0.0 copy-start.1
  360.3 0.5 subtract_convert_fusion
  360.8 0.1 copy.34
  360.9 0.1 copy.35
  360.9 0.6 copy-done.1
  361.6 2.6 fusion.4
  364.2 2.7 fusion.29
  366.9 126.6 %all-gather.15.cloned.1.call-done = bf16[1,1024,5376]{1,2,0:T(8,128)(2,1)} async-done(((bf16[1,1024,336]{1,2,0:T(8,128)(2,1)}), bf16[1,1024,5376]{1,2,0:T(8,128)(2,1)}) %all-gather.15.cloned.1.call-update) | async-done | bytes 11010064 | tf_op jit(solution)/shard_map/all_gather | solution.py:56
  493.5 11.6 %fusion.5 = bf16[256,5376]{1,0:T(8,128)(2,1)S(1)} fusion(bf16[256,1024]{0,1:T(8,128)(2,1)S(1)} %bitcast.66, bf16[1,1024,5376]{1,2,0:T(8,128)(2,1)} %all-gather.15.cloned.1.call-done), kind=kOutput, calls=%fused_computation.7 | convolution fusion | flops 2819948544 | bytes 14286848 | tf_op jit(solution)/shard_map/cond/branch_1_fun/dot_general | solution.py:124
  505.2 2.8 copy.45
  508.0 0.0 reduce-scatter.4.cloned.1.call-update
  508.0 0.7 copy-done.5
  508.7 7.9 %reduce-scatter.4.cloned.1.call-done = bf16[2688,256]{1,0:T(8,128)(2,1)} async-done(((bf16[5376,256]{1,0:T(8,128)(2,1)}), bf16[2688,256]{1,0:T(8,128)(2,1)}) %reduce-scatter.4.cloned.1.call-update) | async-done | bytes 1376272
  516.7 1.8 copy.46
  518.5 0.4 fusion.16
  518.8 2.5 psum.6
  521.3 3.1 fusion.20
  (18 shorter events, 0.3 us)
Async XLA Ops:
  6.5 93.6 %copy-start = (bf16[256,5376]{1,0:T(8,128)(2,1)S(1)}, bf16[256,5376]{1,0:T(8,128)(2,1)}, u32[]{:S(2)}) copy-start(bf16[256,5376]{1,0:T(8,128)(2,1)} %param.7) | copy-start | bytes 8257540
  6.5 93.6 %all-gather.9.cloned.1.call-start = ((), (), s32[]{:S(2)}) async-start(), calls=%async_computation.1 | async-start | bytes 5849088 | tf_op jit(solution)/shard_map/all_gather | solution.py:53
  7.3 181.4 %all-gather.11.cloned.1.call-start = ((), (), s32[]{:S(2)}) async-start(), calls=%async_computation.2 | async-start | bytes 5849088 | tf_op jit(solution)/shard_map/all_gather | solution.py:54
  8.0 344.4 %all-gather.13.cloned.1.call-start = ((), (), s32[]{:S(2)}) async-start(), calls=%async_computation.3 | async-start | bytes 11698176 | tf_op jit(solution)/shard_map/all_gather | solution.py:52
  8.7 484.8 %all-gather.15.cloned.1.call-start = ((), (), s32[]{:S(2)}) async-start(), calls=%async_computation.4 | async-start | bytes 11698176 | tf_op jit(solution)/shard_map/all_gather | solution.py:56
  9.3 507.4 %reduce-scatter.4.cloned.1.call-start = ((), (), s32[]{:S(2)}) async-start(), calls=%async_computation.5 | async-start | bytes 4128768
  10.2 89.9 %copy-start.3 = (f32[5376]{0:T(1024)}, f32[5376]{0:T(1024)S(1)}, u32[]{:S(2)}) copy-start(f32[5376]{0:T(1024)S(1)} %convert_reduce_fusion) | copy-start | bytes 64516
  192.9 18.4 %collective-permute-start = (bf16[256,1024]{1,0:T(8,128)(2,1)S(1)}, bf16[256,1024]{1,0:T(8,128)(2,1)S(1)}, u32[]{:S(2)}, u32[]{:S(2)}) collective-permute-start(bf16[256,1024]{1,0:T(8,128)(2,1)S(1)} %pad_maximum_fusion), channel_id=1, source_target_pairs={{0,2},{2,4},{4,6},{6,8},{8,10},{10,12},{12,14},{14,16},{16,18},{18... | collective-permute-start | bytes 1572872 | tf_op jit(solution)/shard_map/ppermute | solution.py:18
  211.3 13.7 %collective-permute-start.1 = (bf16[256,1024]{1,0:T(8,128)(2,1)S(1)}, bf16[256,1024]{1,0:T(8,128)(2,1)S(1)}, u32[]{:S(2)}, u32[]{:S(2)}) collective-permute-start(bf16[256,1024]{1,0:T(8,128)(2,1)S(1)} %collective-permute-done), channel_id=1, source_target_pairs={{0,2},{2,4},{4,6},{6,8},{8,10},{10,12},{12,14},{14,16},{16,18},{18... | collective-permute-start | bytes 1572872 | tf_op jit(solution)/shard_map/ppermute | solution.py:18
  225.0 25.1 %collective-permute-start.2 = (bf16[256,1024]{1,0:T(8,128)(2,1)S(1)}, bf16[256,1024]{1,0:T(8,128)(2,1)}, u32[]{:S(2)}, u32[]{:S(2)}) collective-permute-start(bf16[256,1024]{1,0:T(8,128)(2,1)S(1)} %collective-permute-done.1), channel_id=1, source_target_pairs={{0,2},{2,4},{4,6},{6,8},{8,10},{10,12},{12,14},{14,16},{16,18},{18... | collective-permute-start | bytes 1572872 | tf_op jit(solution)/shard_map/ppermute | solution.py:18
  250.1 18.7 %collective-permute-start.3 = (bf16[256,1024]{1,0:T(8,128)(2,1)}, bf16[256,1024]{1,0:T(8,128)(2,1)S(1)}, u32[]{:S(2)}, u32[]{:S(2)}) collective-permute-start(bf16[256,1024]{1,0:T(8,128)(2,1)} %collective-permute-done.2), channel_id=1, source_target_pairs={{0,2},{2,4},{4,6},{6,8},{8,10},{10,12},{12,14},{14,16},{16,18},{18... | collective-permute-start | bytes 1572872 | tf_op jit(solution)/shard_map/ppermute | solution.py:18
  271.3 81.1 %copy-start.4 = (f32[5376]{0:T(1024)S(1)}, f32[5376]{0:T(1024)}, u32[]{:S(2)}) copy-start(f32[5376]{0:T(1024)} %copy-done.3) | copy-start | bytes 64516
  360.3 1.3 copy-start.1
  361.6 2.6 copy-start.2
  508.0 0.7 copy-start.5
Sparse Core Ops, SparseCore 0:
  10.2 89.9 all-gather.8
  102.9 85.6 all-gather.10
  191.4 160.9 all-gather.12
  355.1 138.3 all-gather.14
  508.2 8.4 reduce-scatter.3
where the time goes:
time: 532 us; the launch traced here: 531 us
  waiting for transfers between devices  439 us (83%)
  matrix products  32.9 us (6%)
  starting transfers between devices  17.8 us (3%)
  local copies, waits for them, and re-layouts  15.2 us (3%)
  between operations  13.4 us (3%)
  other arithmetic  10.6 us (2%)
    all_gather x1, waiting for transfers between devices, body(): output_full = lax.all_gather(output_weight[0], 'seq', axis=1, tiled=True)  127 us
    all_gather x1, waiting for transfers between devices, body(): lax.all_gather(key_weight[0], 'seq', axis=0, tiled=True)  86.9 us
    all_gather x1, waiting for transfers between devices, body(): lax.all_gather(value_weight[0], 'seq', axis=0, tiled=True)  80.6 us
    all_gather x1, waiting for transfers between devices, body(): lax.all_gather(query_weight[0], 'seq', axis=0, tiled=True)  76.1 us
    ppermute x4, waiting for transfers between devices, from_behind(): return lax.ppermute(block, axis, route)  57.8 us
    ppermute x4, starting transfers between devices, from_behind(): return lax.ppermute(block, axis, route)  17.7 us
    dot_general x1, matrix products, attend_rows(): return jnp.dot(attended, output_full, preferred_element_type=jnp.float32)  11.6 us
  transfers between devices with their start and end apart: 9, of which 9 were waited for; matrix products, arithmetic and copies ran while one was open for 7% of the time, Pallas kernels for 0%

commit v1 on v0

--- a/solution.py
+++ b/solution.py
@@ -10,6 +10,21 @@
 WINDOW = 1024
 QSCALE = 168
 NORM_EPS = 1e-06
+
+
+def advance_digits(v0, axis_tag):
+    newest, lower, r2 = (jax.lax.axis_size(axis_tag), jax.lax.axis_index(axis_tag), v0.shape[0])
+    response = jnp.zeros((*v0.shape[:0], newest * r2, *v0.shape[1:]), v0.dtype)
+    long_array = v0
+    rows = tuple(((ix, (ix + 1) % newest) for ix in range(newest)))
+    jj = 0
+    while jj < newest:
+        z2 = (lower - jj) % newest
+        response = lax.dynamic_update_slice_in_dim(response, long_array, z2 * r2, axis=0)
+        if jj < newest - 1:
+            long_array = jax.lax.ppermute(long_array, axis_tag, rows)
+        jj = jj + 1
+    return response
 
 
 def from_behind(block, axis, distance):
@@ -50,7 +65,7 @@
     section_index = lax.axis_index("section")
     query_full, key_full, value_full = (
         lax.all_gather(query_weight[0], "seq", axis=0, tiled=True),
-        lax.all_gather(key_weight[0], "seq", axis=0, tiled=True),
+        advance_digits(key_weight[0], "seq"),
         lax.all_gather(value_weight[0], "seq", axis=0, tiled=True),
     )
     output_full = lax.all_gather(output_weight[0], "seq", axis=1, tiled=True)

time: 532 us -> 514 us (0.966)
  waiting for transfers between devices: 439 us -> 413 us
  local copies, waits for them, and re-layouts: 15.2 us -> 24 us
    ppermute x0 -> x15, waiting for transfers between devices: none -> 262 us  [advance_digits(): long_array = jax.lax.ppermute(long_array, axis_tag, rows)]
    all_gather x1 -> x0, waiting for transfers between devices: 86.9 us -> none  [body(): lax.all_gather(key_weight[0], 'seq', axis=0, tiled=True)]
    all_gather x1, waiting for transfers between devices: 80.6 us -> 0.02 us  [body(): lax.all_gather(value_weight[0], 'seq', axis=0, tiled=True)]
    all_gather x1, waiting for transfers between devices: 76.1 us -> 0.01 us  [body(): lax.all_gather(query_weight[0], 'seq', axis=0, tiled=True)]
    ppermute x4, waiting for transfers between devices: 57.8 us -> 33.5 us  [from_behind(): return lax.ppermute(block, axis, route)]
    all_gather x1, waiting for transfers between devices: 127 us -> 107 us  [body(): output_full = lax.all_gather(output_weight[0], 'seq', axis=1, tiled=True)]
    dynamic_update_slice x0 -> x16, local copies, waits for them, and re-layouts: none -> 7.3 us  [advance_digits(): lax.dynamic_update_slice_in_dim(response, long_array, z2 * r2, axis=0)]
    unnamed x6 -> x5, waiting for transfers between devices: 10.6 us -> 10.8 us
  transfers between devices with their start and end apart: 9 -> 23, of which waited for: 9 -> 21; matrix products, arithmetic and copies ran while one was open for 7% -> 8% of each run, Pallas kernels for 0% -> 0%
where the time goes in v1:
time: 514 us; the launch traced here: 513 us
  waiting for transfers between devices  413 us (80%)
  matrix products  30.9 us (6%)
  local copies, waits for them, and re-layouts  24 us (5%)
  starting transfers between devices  18.8 us (4%)
  between operations  13.7 us (3%)
  other arithmetic  9.79 us (2%)
    ppermute x15, waiting for transfers between devices, advance_digits(): long_array = jax.lax.ppermute(long_array, axis_tag, rows)  262 us
    all_gather x1, waiting for transfers between devices, body(): output_full = lax.all_gather(output_weight[0], 'seq', axis=1, tiled=True)  107 us
    ppermute x4, waiting for transfers between devices, from_behind(): return lax.ppermute(block, axis, route)  33.5 us
    ppermute x4, starting transfers between devices, from_behind(): return lax.ppermute(block, axis, route)  15.6 us
    dot_general x1, matrix products, attend_rows(): return jnp.dot(attended, output_full, preferred_element_type=jnp.float32)  11.6 us
    unnamed x5, waiting for transfers between devices  10.8 us
  transfers between devices with their start and end apart: 23, of which 21 were waited for; matrix products, arithmetic and copies ran while one was open for 8% of the time, Pallas kernels for 0%

profile of v1, /device:TPU:0, one launch (start us, length us, event | category | flops | bytes accessed | tf_op | source)
XLA Modules:
  0.0 512.9 jit_solution(8479669559525064834)
XLA Ops:
  6.5 0.7 all-gather.7.cloned.1.call-update
  7.3 0.7 all-gather.9.cloned.1.call-update
  8.1 0.7 all-gather.11.cloned.1.call-update
  8.8 3.0 collective-permute-start
  11.8 12.3 %collective-permute-done = bf16[336,512]{1,0:T(8,128)(2,1)S(1)} collective-permute-done((bf16[336,512]{1,0:T(8,128)(2,1)}, bf16[336,512]{1,0:T(8,128)(2,1)S(1)}, u32[]{:S(2)}, u32[]{:S(2)}) %collective-permute-start) | collective-permute-done | bytes 344096 | tf_op jit(solution)/shard_map/ppermute | solution.py:25
  24.1 0.7 copy-done.4
  24.8 18.0 %collective-permute-done.1 = bf16[336,512]{1,0:T(8,128)(2,1)S(1)} collective-permute-done((bf16[336,512]{1,0:T(8,128)(2,1)S(1)}, bf16[336,512]{1,0:T(8,128)(2,1)S(1)}, u32[]{:S(2)}, u32[]{:S(2)}) %collective-permute-start.1) | collective-permute-done | bytes 344096 | tf_op jit(solution)/shard_map/ppermute | solution.py:25
  42.8 21.0 %collective-permute-done.2 = bf16[336,512]{1,0:T(8,128)(2,1)} collective-permute-done((bf16[336,512]{1,0:T(8,128)(2,1)S(1)}, bf16[336,512]{1,0:T(8,128)(2,1)}, u32[]{:S(2)}, u32[]{:S(2)}) %collective-permute-start.2) | collective-permute-done | bytes 344096 | tf_op jit(solution)/shard_map/ppermute | solution.py:25
  63.8 14.4 %collective-permute-done.3 = bf16[336,512]{1,0:T(8,128)(2,1)S(1)} collective-permute-done((bf16[336,512]{1,0:T(8,128)(2,1)}, bf16[336,512]{1,0:T(8,128)(2,1)S(1)}, u32[]{:S(2)}, u32[]{:S(2)}) %collective-permute-start.3) | collective-permute-done | bytes 344096 | tf_op jit(solution)/shard_map/ppermute | solution.py:25
  78.2 0.7 copy-done.7
  78.9 20.6 %collective-permute-done.4 = bf16[336,512]{1,0:T(8,128)(2,1)S(1)} collective-permute-done((bf16[336,512]{1,0:T(8,128)(2,1)S(1)}, bf16[336,512]{1,0:T(8,128)(2,1)S(1)}, u32[]{:S(2)}, u32[]{:S(2)}) %collective-permute-start.4) | collective-permute-done | bytes 344096 | tf_op jit(solution)/shard_map/ppermute | solution.py:25
  99.5 17.1 %collective-permute-done.5 = bf16[336,512]{1,0:T(8,128)(2,1)S(1)} collective-permute-done((bf16[336,512]{1,0:T(8,128)(2,1)S(1)}, bf16[336,512]{1,0:T(8,128)(2,1)S(1)}, u32[]{:S(2)}, u32[]{:S(2)}) %collective-permute-start.5) | collective-permute-done | bytes 344096 | tf_op jit(solution)/shard_map/ppermute | solution.py:25
  116.6 0.7 copy-done.6
  117.4 14.8 %collective-permute-done.6 = bf16[336,512]{1,0:T(8,128)(2,1)S(1)} collective-permute-done((bf16[336,512]{1,0:T(8,128)(2,1)S(1)}, bf16[336,512]{1,0:T(8,128)(2,1)S(1)}, u32[]{:S(2)}, u32[]{:S(2)}) %collective-permute-start.6) | collective-permute-done | bytes 344096 | tf_op jit(solution)/shard_map/ppermute | solution.py:25
  132.2 15.4 %collective-permute-done.7 = bf16[336,512]{1,0:T(8,128)(2,1)S(1)} collective-permute-done((bf16[336,512]{1,0:T(8,128)(2,1)S(1)}, bf16[336,512]{1,0:T(8,128)(2,1)S(1)}, u32[]{:S(2)}, u32[]{:S(2)}) %collective-permute-start.7) | collective-permute-done | bytes 344096 | tf_op jit(solution)/shard_map/ppermute | solution.py:25
  147.6 0.5 multiply_cosine_fusion
  148.2 2.4 fusion.8
  150.6 16.4 %collective-permute-done.8 = bf16[336,512]{1,0:T(8,128)(2,1)} collective-permute-done((bf16[336,512]{1,0:T(8,128)(2,1)S(1)}, bf16[336,512]{1,0:T(8,128)(2,1)}, u32[]{:S(2)}, u32[]{:S(2)}) %collective-permute-start.8) | collective-permute-done | bytes 344096 | tf_op jit(solution)/shard_map/ppermute | solution.py:25
  167.0 0.4 broadcast_in_dim.6
  167.4 20.1 %collective-permute-done.9 = bf16[336,512]{1,0:T(8,128)(2,1)} collective-permute-done((bf16[336,512]{1,0:T(8,128)(2,1)}, bf16[336,512]{1,0:T(8,128)(2,1)}, u32[]{:S(2)}, u32[]{:S(2)}) %collective-permute-start.9) | collective-permute-done | bytes 344096 | tf_op jit(solution)/shard_map/ppermute | solution.py:25
  187.8 21.1 %collective-permute-done.10 = bf16[336,512]{1,0:T(8,128)(2,1)S(1)} collective-permute-done((bf16[336,512]{1,0:T(8,128)(2,1)}, bf16[336,512]{1,0:T(8,128)(2,1)S(1)}, u32[]{:S(2)}, u32[]{:S(2)}) %collective-permute-start.10) | collective-permute-done | bytes 344096 | tf_op jit(solution)/shard_map/ppermute | solution.py:25
  208.8 1.0 constant_dynamic-update-slice_fusion.17
  209.8 1.0 constant_dynamic-update-slice_fusion.16
  210.8 1.0 constant_dynamic-update-slice_fusion.15
  211.9 13.8 %collective-permute-done.11 = bf16[336,512]{1,0:T(8,128)(2,1)S(1)} collective-permute-done((bf16[336,512]{1,0:T(8,128)(2,1)S(1)}, bf16[336,512]{1,0:T(8,128)(2,1)S(1)}, u32[]{:S(2)}, u32[]{:S(2)}) %collective-permute-start.11) | collective-permute-done | bytes 344096 | tf_op jit(solution)/shard_map/ppermute | solution.py:25
  225.6 1.0 constant_dynamic-update-slice_fusion.14
  226.7 1.0 constant_dynamic-update-slice_fusion.13
  227.7 19.6 %collective-permute-done.12 = bf16[336,512]{1,0:T(8,128)(2,1)S(1)} collective-permute-done((bf16[336,512]{1,0:T(8,128)(2,1)S(1)}, bf16[336,512]{1,0:T(8,128)(2,1)S(1)}, u32[]{:S(2)}, u32[]{:S(2)}) %collective-permute-start.12) | collective-permute-done | bytes 344096 | tf_op jit(solution)/shard_map/ppermute | solution.py:25
  247.3 1.0 constant_dynamic-update-slice_fusion.11
  248.3 1.0 constant_dynamic-update-slice_fusion.10
  249.4 19.3 %collective-permute-done.13 = bf16[336,512]{1,0:T(8,128)(2,1)S(1)} collective-permute-done((bf16[336,512]{1,0:T(8,128)(2,1)S(1)}, bf16[336,512]{1,0:T(8,128)(2,1)S(1)}, u32[]{:S(2)}, u32[]{:S(2)}) %collective-permute-start.13) | collective-permute-done | bytes 344096 | tf_op jit(solution)/shard_map/ppermute | solution.py:25
  268.8 18.0 %collective-permute-done.14 = bf16[336,512]{1,0:T(8,128)(2,1)S(1)} collective-permute-done((bf16[336,512]{1,0:T(8,128)(2,1)S(1)}, bf16[336,512]{1,0:T(8,128)(2,1)S(1)}, u32[]{:S(2)}, u32[]{:S(2)}) %collective-permute-start.14) | collective-permute-done | bytes 344096 | tf_op jit(solution)/shard_map/ppermute | solution.py:25
  286.9 2.5 fusion.39
  289.4 1.2 reshape.109
  290.6 0.3 multiply_reduce_fusion.1
  291.3 0.5 subtract_convert_fusion.1
  291.9 0.4 pad_maximum_fusion.1
  292.3 4.2 fusion.28
  296.6 1.3 collective-permute-start.15
  297.9 9.5 %collective-permute-done.15 = bf16[256,1024]{1,0:T(8,128)(2,1)S(1)} collective-permute-done((bf16[256,1024]{1,0:T(8,128)(2,1)S(1)}, bf16[256,1024]{1,0:T(8,128)(2,1)S(1)}, u32[]{:S(2)}, u32[]{:S(2)}) %collective-permute-start.15) | collective-permute-done | bytes 524320 | tf_op jit(solution)/shard_map/ppermute | solution.py:33
  307.4 4.4 collective-permute-start.16
  311.8 10.3 %collective-permute-done.16 = bf16[256,1024]{1,0:T(8,128)(2,1)S(1)} collective-permute-done((bf16[256,1024]{1,0:T(8,128)(2,1)S(1)}, bf16[256,1024]{1,0:T(8,128)(2,1)S(1)}, u32[]{:S(2)}, u32[]{:S(2)}) %collective-permute-start.16) | collective-permute-done | bytes 524320 | tf_op jit(solution)/shard_map/ppermute | solution.py:33
  322.1 5.2 %collective-permute-start.17 = (bf16[256,1024]{1,0:T(8,128)(2,1)S(1)}, bf16[256,1024]{1,0:T(8,128)(2,1)}, u32[]{:S(2)}, u32[]{:S(2)}) collective-permute-start(bf16[256,1024]{1,0:T(8,128)(2,1)S(1)} %collective-permute-done.16), channel_id=1, source_target_pairs={{0,2},{2,4},{4,6},{6,8},{8,10},{10,12},{12,14},{14,16},{16,18},{18... | collective-permute-start | bytes 1572872 | tf_op jit(solution)/shard_map/ppermute | solution.py:33
  327.3 7.3 %collective-permute-done.17 = bf16[256,1024]{1,0:T(8,128)(2,1)} collective-permute-done((bf16[256,1024]{1,0:T(8,128)(2,1)S(1)}, bf16[256,1024]{1,0:T(8,128)(2,1)}, u32[]{:S(2)}, u32[]{:S(2)}) %collective-permute-start.17) | collective-permute-done | bytes 524320 | tf_op jit(solution)/shard_map/ppermute | solution.py:33
  334.6 4.7 collective-permute-start.18
  339.4 0.4 fusion.26
  339.8 6.4 %collective-permute-done.18 = bf16[256,1024]{1,0:T(8,128)(2,1)S(1)} collective-permute-done((bf16[256,1024]{1,0:T(8,128)(2,1)}, bf16[256,1024]{1,0:T(8,128)(2,1)S(1)}, u32[]{:S(2)}, u32[]{:S(2)}) %collective-permute-start.18) | collective-permute-done | bytes 524320 | tf_op jit(solution)/shard_map/ppermute | solution.py:33
  346.2 1.1 constant_dynamic-update-slice_fusion.3
  347.4 1.2 fusion.41
  348.6 3.6 reshape.110
  352.2 1.4 copy.44
  353.6 7.3 %fusion.19 = f32[32,8,8,128]{3,1,2,0:T(8,128)S(1)} fusion(bf16[1,5376,1024]{2,1,0:T(8,128)(2,1)} %all-gather.9.cloned.1.call-done, bf16[256,5376]{1,0:T(8,128)(2,1)} %param.7, f32[5376]{0:T(1024)S(1)} %copy-done.15, f32[256]{0:T(256)S(1)} %add_rsqrt_fusion.3), kind=kOutput, calls=%fused_computation.25 | convolution fusion | flops 2824077312 | bytes 14833664 | tf_op jit(solution)/shard_map/cond/branch_1_fun/dot_general | solution.py:98
  361.1 0.3 multiply_reduce_fusion
  362.0 0.5 subtract_convert_fusion
  363.0 2.6 fusion.4
  365.6 2.7 fusion.27
  368.3 107.1 %all-gather.11.cloned.1.call-done = bf16[1,1024,5376]{1,2,0:T(8,128)(2,1)} async-done(((bf16[1,1024,336]{1,2,0:T(8,128)(2,1)}), bf16[1,1024,5376]{1,2,0:T(8,128)(2,1)}) %all-gather.11.cloned.1.call-update) | async-done | bytes 11010064 | tf_op jit(solution)/shard_map/all_gather | solution.py:71
  475.5 11.6 %fusion.5 = bf16[256,5376]{1,0:T(8,128)(2,1)S(1)} fusion(bf16[256,1024]{0,1:T(8,128)(2,1)S(1)} %bitcast.67, bf16[1,1024,5376]{1,2,0:T(8,128)(2,1)} %all-gather.11.cloned.1.call-done), kind=kOutput, calls=%fused_computation.7 | convolution fusion | flops 2819948544 | bytes 14286848 | tf_op jit(solution)/shard_map/cond/branch_1_fun/dot_general | solution.py:139
  487.1 2.8 copy.45
  490.0 8.7 %reduce-scatter.4.cloned.1.call-done = bf16[2688,256]{1,0:T(8,128)(2,1)} async-done(((bf16[5376,256]{1,0:T(8,128)(2,1)}), bf16[2688,256]{1,0:T(8,128)(2,1)}) %reduce-scatter.4.cloned.1.call-update) | async-done | bytes 1376272
  498.7 1.8 copy.46
  500.5 0.4 fusion.14
  500.8 2.5 psum.6
  503.3 3.1 fusion.18
  (86 shorter events, 2.5 us)
Async XLA Ops:
  6.5 160.8 %copy-start.3 = (bf16[1,336,512]{2,1,0:T(8,128)(2,1)S(1)}, bf16[1,336,512]{2,1,0:T(8,128)(2,1)}, u32[]{:S(2)}) copy-start(bf16[1,336,512]{2,1,0:T(8,128)(2,1)} %param.9) | copy-start | bytes 1032196
  6.5 285.8 %all-gather.7.cloned.1.call-start = ((), (), s32[]{:S(2)}) async-start(), calls=%async_computation.1 | async-start | bytes 5849088 | tf_op jit(solution)/shard_map/all_gather | solution.py:69
  7.3 180.3 %copy-start.16 = (bf16[1,5376]{1,0:T(2,128)(2,1)S(1)}, bf16[1,5376]{1,0:T(2,128)(2,1)}, u32[]{:S(2)}) copy-start(bf16[1,5376]{1,0:T(2,128)(2,1)} %param.12) | copy-start | bytes 32260
  7.3 346.3 %all-gather.9.cloned.1.call-start = ((), (), s32[]{:S(2)}) async-start(), calls=%async_computation.2 | async-start | bytes 11698176 | tf_op jit(solution)/shard_map/all_gather | solution.py:67
  8.0 467.4 %all-gather.11.cloned.1.call-start = ((), (), s32[]{:S(2)}) async-start(), calls=%async_computation.3 | async-start | bytes 11698176 | tf_op jit(solution)/shard_map/all_gather | solution.py:71
  8.8 489.9 %reduce-scatter.4.cloned.1.call-start = ((), (), s32[]{:S(2)}) async-start(), calls=%async_computation.4 | async-start | bytes 4128768
  8.8 15.3 %collective-permute-start = (bf16[336,512]{1,0:T(8,128)(2,1)}, bf16[336,512]{1,0:T(8,128)(2,1)S(1)}, u32[]{:S(2)}, u32[]{:S(2)}) collective-permute-start(bf16[336,512]{1,0:T(8,128)(2,1)} %bitcast.64), channel_id=1, source_target_pairs={{0,2},{2,4},{4,6},{6,8},{8,10},{10,12},{12,14},{14,16},{16,18},{18... | collective-permute-start | bytes 1032200 | tf_op jit(solution)/shard_map/ppermute | solution.py:25
  24.1 0.7 copy-start.4
  24.8 18.0 %collective-permute-start.1 = (bf16[336,512]{1,0:T(8,128)(2,1)S(1)}, bf16[336,512]{1,0:T(8,128)(2,1)S(1)}, u32[]{:S(2)}, u32[]{:S(2)}) collective-permute-start(bf16[336,512]{1,0:T(8,128)(2,1)S(1)} %collective-permute-done), channel_id=1, source_target_pairs={{0,2},{2,4},{4,6},{6,8},{8,10},{10,12},{12,14},{14,16},{16,18},{18... | collective-permute-start | bytes 1032200 | tf_op jit(solution)/shard_map/ppermute | solution.py:25
  42.8 89.4 %copy-start.8 = (bf16[336,512]{1,0:T(8,128)(2,1)}, bf16[336,512]{1,0:T(8,128)(2,1)S(1)}, u32[]{:S(2)}) copy-start(bf16[336,512]{1,0:T(8,128)(2,1)S(1)} %collective-permute-done.1) | copy-start | bytes 1032196
  42.8 21.0 %collective-permute-start.2 = (bf16[336,512]{1,0:T(8,128)(2,1)S(1)}, bf16[336,512]{1,0:T(8,128)(2,1)}, u32[]{:S(2)}, u32[]{:S(2)}) collective-permute-start(bf16[336,512]{1,0:T(8,128)(2,1)S(1)} %collective-permute-done.1), channel_id=1, source_target_pairs={{0,2},{2,4},{4,6},{6,8},{8,10},{10,12},{12,14},{14,16},{16,18},{18... | collective-permute-start | bytes 1032200 | tf_op jit(solution)/shard_map/ppermute | solution.py:25
  63.8 14.4 %collective-permute-start.3 = (bf16[336,512]{1,0:T(8,128)(2,1)}, bf16[336,512]{1,0:T(8,128)(2,1)S(1)}, u32[]{:S(2)}, u32[]{:S(2)}) collective-permute-start(bf16[336,512]{1,0:T(8,128)(2,1)} %collective-permute-done.2), channel_id=1, source_target_pairs={{0,2},{2,4},{4,6},{6,8},{8,10},{10,12},{12,14},{14,16},{16,18},{18... | collective-permute-start | bytes 1032200 | tf_op jit(solution)/shard_map/ppermute | solution.py:25
  78.2 0.7 copy-start.7
  78.2 21.3 %collective-permute-start.4 = (bf16[336,512]{1,0:T(8,128)(2,1)S(1)}, bf16[336,512]{1,0:T(8,128)(2,1)S(1)}, u32[]{:S(2)}, u32[]{:S(2)}) collective-permute-start(bf16[336,512]{1,0:T(8,128)(2,1)S(1)} %collective-permute-done.3), channel_id=1, source_target_pairs={{0,2},{2,4},{4,6},{6,8},{8,10},{10,12},{12,14},{14,16},{16,18},{18... | collective-permute-start | bytes 1032200 | tf_op jit(solution)/shard_map/ppermute | solution.py:25
  99.5 32.6 %copy-start.11 = (bf16[336,512]{1,0:T(8,128)(2,1)}, bf16[336,512]{1,0:T(8,128)(2,1)S(1)}, u32[]{:S(2)}) copy-start(bf16[336,512]{1,0:T(8,128)(2,1)S(1)} %collective-permute-done.4) | copy-start | bytes 1032196
  99.5 17.1 %collective-permute-start.5 = (bf16[336,512]{1,0:T(8,128)(2,1)S(1)}, bf16[336,512]{1,0:T(8,128)(2,1)S(1)}, u32[]{:S(2)}, u32[]{:S(2)}) collective-permute-start(bf16[336,512]{1,0:T(8,128)(2,1)S(1)} %collective-permute-done.4), channel_id=1, source_target_pairs={{0,2},{2,4},{4,6},{6,8},{8,10},{10,12},{12,14},{14,16},{16,18},{18... | collective-permute-start | bytes 1032200 | tf_op jit(solution)/shard_map/ppermute | solution.py:25
  116.6 0.7 copy-start.6
  117.4 14.8 %collective-permute-start.6 = (bf16[336,512]{1,0:T(8,128)(2,1)S(1)}, bf16[336,512]{1,0:T(8,128)(2,1)S(1)}, u32[]{:S(2)}, u32[]{:S(2)}) collective-permute-start(bf16[336,512]{1,0:T(8,128)(2,1)S(1)} %collective-permute-done.5), channel_id=1, source_target_pairs={{0,2},{2,4},{4,6},{6,8},{8,10},{10,12},{12,14},{14,16},{16,18},{18... | collective-permute-start | bytes 1032200 | tf_op jit(solution)/shard_map/ppermute | solution.py:25
  132.1 34.8 %copy-start.10 = (bf16[336,512]{1,0:T(8,128)(2,1)}, bf16[336,512]{1,0:T(8,128)(2,1)S(1)}, u32[]{:S(2)}) copy-start(bf16[336,512]{1,0:T(8,128)(2,1)S(1)} %collective-permute-done.6) | copy-start | bytes 1032196
  132.2 15.5 %collective-permute-start.7 = (bf16[336,512]{1,0:T(8,128)(2,1)S(1)}, bf16[336,512]{1,0:T(8,128)(2,1)S(1)}, u32[]{:S(2)}, u32[]{:S(2)}) collective-permute-start(bf16[336,512]{1,0:T(8,128)(2,1)S(1)} %collective-permute-done.6), channel_id=1, source_target_pairs={{0,2},{2,4},{4,6},{6,8},{8,10},{10,12},{12,14},{14,16},{16,18},{18... | collective-permute-start | bytes 1032200 | tf_op jit(solution)/shard_map/ppermute | solution.py:25
  147.6 19.3 %copy-start.12 = (bf16[336,512]{1,0:T(8,128)(2,1)}, bf16[336,512]{1,0:T(8,128)(2,1)S(1)}, u32[]{:S(2)}) copy-start(bf16[336,512]{1,0:T(8,128)(2,1)S(1)} %collective-permute-done.7) | copy-start | bytes 1032196
  147.6 19.3 %collective-permute-start.8 = (bf16[336,512]{1,0:T(8,128)(2,1)S(1)}, bf16[336,512]{1,0:T(8,128)(2,1)}, u32[]{:S(2)}, u32[]{:S(2)}) collective-permute-start(bf16[336,512]{1,0:T(8,128)(2,1)S(1)} %collective-permute-done.7), channel_id=1, source_target_pairs={{0,2},{2,4},{4,6},{6,8},{8,10},{10,12},{12,14},{14,16},{16,18},{18... | collective-permute-start | bytes 1032200 | tf_op jit(solution)/shard_map/ppermute | solution.py:25
  167.0 20.6 %collective-permute-start.9 = (bf16[336,512]{1,0:T(8,128)(2,1)}, bf16[336,512]{1,0:T(8,128)(2,1)}, u32[]{:S(2)}, u32[]{:S(2)}) collective-permute-start(bf16[336,512]{1,0:T(8,128)(2,1)} %collective-permute-done.8), channel_id=1, source_target_pairs={{0,2},{2,4},{4,6},{6,8},{8,10},{10,12},{12,14},{14,16},{16,18},{18... | collective-permute-start | bytes 1032200 | tf_op jit(solution)/shard_map/ppermute | solution.py:25
  167.0 20.7 %copy-start.5 = (bf16[336,512]{1,0:T(8,128)(2,1)S(1)}, bf16[336,512]{1,0:T(8,128)(2,1)}, u32[]{:S(2)}) copy-start(bf16[336,512]{1,0:T(8,128)(2,1)} %copy-done.4) | copy-start | bytes 1032196
  167.0 20.7 %copy-start.9 = (bf16[336,512]{1,0:T(8,128)(2,1)S(1)}, bf16[336,512]{1,0:T(8,128)(2,1)}, u32[]{:S(2)}) copy-start(bf16[336,512]{1,0:T(8,128)(2,1)} %copy-done.8) | copy-start | bytes 1032196
  167.4 60.3 %copy-start.13 = (bf16[336,512]{1,0:T(8,128)(2,1)S(1)}, bf16[336,512]{1,0:T(8,128)(2,1)}, u32[]{:S(2)}) copy-start(bf16[336,512]{1,0:T(8,128)(2,1)} %copy-done.12) | copy-start | bytes 1032196
  167.4 119.5 %copy-start = (bf16[256,5376]{1,0:T(8,128)(2,1)S(1)}, bf16[256,5376]{1,0:T(8,128)(2,1)}, u32[]{:S(2)}) copy-start(bf16[256,5376]{1,0:T(8,128)(2,1)} %param.7) | copy-start | bytes 8257540
  187.6 21.2 %collective-permute-start.10 = (bf16[336,512]{1,0:T(8,128)(2,1)}, bf16[336,512]{1,0:T(8,128)(2,1)S(1)}, u32[]{:S(2)}, u32[]{:S(2)}) collective-permute-start(bf16[336,512]{1,0:T(8,128)(2,1)} %collective-permute-done.9), channel_id=1, source_target_pairs={{0,2},{2,4},{4,6},{6,8},{8,10},{10,12},{12,14},{14,16},{16,18},{18... | collective-permute-start | bytes 1032200 | tf_op jit(solution)/shard_map/ppermute | solution.py:25
  187.7 99.2 %copy-start.14 = (f32[5376]{0:T(1024)}, f32[5376]{0:T(1024)S(1)}, u32[]{:S(2)}) copy-start(f32[5376]{0:T(1024)S(1)} %convert_reduce_fusion) | copy-start | bytes 64516
  208.8 16.8 %collective-permute-start.11 = (bf16[336,512]{1,0:T(8,128)(2,1)S(1)}, bf16[336,512]{1,0:T(8,128)(2,1)S(1)}, u32[]{:S(2)}, u32[]{:S(2)}) collective-permute-start(bf16[336,512]{1,0:T(8,128)(2,1)S(1)} %collective-permute-done.10), channel_id=1, source_target_pairs={{0,2},{2,4},{4,6},{6,8},{8,10},{10,12},{12,14},{14,16},{16,18},{18... | collective-permute-start | bytes 1032200 | tf_op jit(solution)/shard_map/ppermute | solution.py:25
  225.6 21.7 %collective-permute-start.12 = (bf16[336,512]{1,0:T(8,128)(2,1)S(1)}, bf16[336,512]{1,0:T(8,128)(2,1)S(1)}, u32[]{:S(2)}, u32[]{:S(2)}) collective-permute-start(bf16[336,512]{1,0:T(8,128)(2,1)S(1)} %collective-permute-done.11), channel_id=1, source_target_pairs={{0,2},{2,4},{4,6},{6,8},{8,10},{10,12},{12,14},{14,16},{16,18},{18... | collective-permute-start | bytes 1032200 | tf_op jit(solution)/shard_map/ppermute | solution.py:25
  247.3 21.4 %collective-permute-start.13 = (bf16[336,512]{1,0:T(8,128)(2,1)S(1)}, bf16[336,512]{1,0:T(8,128)(2,1)S(1)}, u32[]{:S(2)}, u32[]{:S(2)}) collective-permute-start(bf16[336,512]{1,0:T(8,128)(2,1)S(1)} %collective-permute-done.12), channel_id=1, source_target_pairs={{0,2},{2,4},{4,6},{6,8},{8,10},{10,12},{12,14},{14,16},{16,18},{18... | collective-permute-start | bytes 1032200 | tf_op jit(solution)/shard_map/ppermute | solution.py:25
  268.7 18.1 %collective-permute-start.14 = (bf16[336,512]{1,0:T(8,128)(2,1)S(1)}, bf16[336,512]{1,0:T(8,128)(2,1)S(1)}, u32[]{:S(2)}, u32[]{:S(2)}) collective-permute-start(bf16[336,512]{1,0:T(8,128)(2,1)S(1)} %collective-permute-done.13), channel_id=1, source_target_pairs={{0,2},{2,4},{4,6},{6,8},{8,10},{10,12},{12,14},{14,16},{16,18},{18... | collective-permute-start | bytes 1032200 | tf_op jit(solution)/shard_map/ppermute | solution.py:25
  296.6 10.8 %collective-permute-start.15 = (bf16[256,1024]{1,0:T(8,128)(2,1)S(1)}, bf16[256,1024]{1,0:T(8,128)(2,1)S(1)}, u32[]{:S(2)}, u32[]{:S(2)}) collective-permute-start(bf16[256,1024]{1,0:T(8,128)(2,1)S(1)} %pad_maximum_fusion), channel_id=1, source_target_pairs={{0,2},{2,4},{4,6},{6,8},{8,10},{10,12},{12,14},{14,16},{16,18},{18... | collective-permute-start | bytes 1572872 | tf_op jit(solution)/shard_map/ppermute | solution.py:33
  307.4 14.7 %collective-permute-start.16 = (bf16[256,1024]{1,0:T(8,128)(2,1)S(1)}, bf16[256,1024]{1,0:T(8,128)(2,1)S(1)}, u32[]{:S(2)}, u32[]{:S(2)}) collective-permute-start(bf16[256,1024]{1,0:T(8,128)(2,1)S(1)} %collective-permute-done.15), channel_id=1, source_target_pairs={{0,2},{2,4},{4,6},{6,8},{8,10},{10,12},{12,14},{14,16},{16,18},{18... | collective-permute-start | bytes 1572872 | tf_op jit(solution)/shard_map/ppermute | solution.py:33
  322.1 12.5 %collective-permute-start.17 = (bf16[256,1024]{1,0:T(8,128)(2,1)S(1)}, bf16[256,1024]{1,0:T(8,128)(2,1)}, u32[]{:S(2)}, u32[]{:S(2)}) collective-permute-start(bf16[256,1024]{1,0:T(8,128)(2,1)S(1)} %collective-permute-done.16), channel_id=1, source_target_pairs={{0,2},{2,4},{4,6},{6,8},{8,10},{10,12},{12,14},{14,16},{16,18},{18... | collective-permute-start | bytes 1572872 | tf_op jit(solution)/shard_map/ppermute | solution.py:33
  334.6 11.5 %collective-permute-start.18 = (bf16[256,1024]{1,0:T(8,128)(2,1)}, bf16[256,1024]{1,0:T(8,128)(2,1)S(1)}, u32[]{:S(2)}, u32[]{:S(2)}) collective-permute-start(bf16[256,1024]{1,0:T(8,128)(2,1)} %collective-permute-done.17), channel_id=1, source_target_pairs={{0,2},{2,4},{4,6},{6,8},{8,10},{10,12},{12,14},{14,16},{16,18},{18... | collective-permute-start | bytes 1572872 | tf_op jit(solution)/shard_map/ppermute | solution.py:33
  347.4 6.2 %copy-start.15 = (f32[5376]{0:T(1024)S(1)}, f32[5376]{0:T(1024)}, u32[]{:S(2)}) copy-start(f32[5376]{0:T(1024)} %copy-done.14) | copy-start | bytes 64516
  361.7 1.3 copy-start.1
  363.0 2.6 copy-start.2
  487.1 2.9 copy-start.17
Sparse Core Ops, SparseCore 0:
  10.2 113.6 all-gather.6
  126.6 177.7 all-gather.8
  307.2 168.2 all-gather.10
  490.1 8.5 reduce-scatter.3
